TPU v7x, 256 devices: a whole 4x4x8 slice. The times are simulated.
256 devices in a mesh: wide: 32 (over z, y), tp: 8 (over x, core).
Axes of the slice: x: 4, y: 4, z: 8, core: 2. Of those that a mesh axis runs over, the one named last changes fastest.
Arguments:
- queries: bfloat16 [16384, 8192], P('wide', 'tp'), may hold values from -8 to 8
- resp_kv: bfloat16 [2, 16384, 1024], P(None, 'wide', 'tp'), may hold values from -8 to 8
- prompt_kv: bfloat16 [2, 65536, 1024], P(None, 'wide', 'tp'), may hold values from -6 to 6
- out_weight: bfloat16 [8192, 4096], P('tp'), may hold values from -0.0625 to 0.0625
- lengths: int32 [128, 4], P('wide'), may hold values from 1 to 64, 128 in all within a row
- group_prompt: int32 [32, 4], P('wide'), may hold values from 0 to 31, as said below
Outputs:
- projected: bfloat16 [16384, 4096], P(('wide', 'tp'))
Inputs may be any that keep to these rules, and one draw needn't show every extreme that they name: `group_prompt`: the 4 blocks of index w belong to the prompts w, w - 1, ..., w - 4 + 1 modulo 32, one each, in an order drawn for each w.
All inputs are finite; a program needn't handle non-finite values.
Results may differ from a plain program's by a relative error of at most 0.018.
Values may be sent and summed in bfloat16 or wider, within the bound.
A program may use at most 64 MiB of HBM per device.

v0:
```python
import math

import jax
import jax.numpy as jnp
from jax import lax
from jax.sharding import PartitionSpec as P

HEAD_DIM = 128


def from_behind(value, axis, steps):
    count = lax.axis_size(axis)
    pairs = [(source, (source + steps) % count) for source in range(count)]
    return lax.ppermute(value, axis, pairs)


def attend_block(query_rows, prompt_pair, self_pair, run_lengths):
    run_len = query_rows.shape[0]
    kv_width = prompt_pair.shape[2]
    kv_heads = kv_width // HEAD_DIM
    group_size = query_rows.shape[1] // kv_width
    query_heads = query_rows.reshape(run_len, kv_heads, group_size, HEAD_DIM)
    prompt_keys = prompt_pair[0].reshape(-1, kv_heads, HEAD_DIM)
    prompt_vals = prompt_pair[1].reshape(-1, kv_heads, HEAD_DIM)
    self_keys = self_pair[0].reshape(-1, kv_heads, HEAD_DIM)
    self_vals = self_pair[1].reshape(-1, kv_heads, HEAD_DIM)
    score_scale = 1.0 / math.sqrt(HEAD_DIM)
    prompt_score = (
        jnp.einsum("tkgd,skd->kgts", query_heads, prompt_keys, preferred_element_type=jnp.float32)
        * score_scale
    )
    self_score = (
        jnp.einsum("tkgd,skd->kgts", query_heads, self_keys, preferred_element_type=jnp.float32)
        * score_scale
    )
    boundary = jnp.cumsum(run_lengths)
    position = jnp.arange(run_len, dtype=jnp.int32)
    segment = jnp.sum((position[:, None] >= boundary[None, :]).astype(jnp.int32), axis=1)
    allowed = (segment[:, None] == segment[None, :]) & (position[None, :] <= position[:, None])
    self_score = jnp.where(allowed, self_score, -jnp.inf)
    highest = jnp.maximum(jnp.max(prompt_score, axis=-1), jnp.max(self_score, axis=-1))[..., None]
    prompt_exp = jnp.exp(prompt_score - highest)
    self_exp = jnp.exp(self_score - highest)
    total_weight = jnp.sum(prompt_exp, axis=-1, keepdims=True) + jnp.sum(
        self_exp, axis=-1, keepdims=True
    )
    prompt_weight = (prompt_exp / total_weight).astype(jnp.bfloat16)
    self_weight = (self_exp / total_weight).astype(jnp.bfloat16)
    mixed = jnp.einsum(
        "kgts,skd->tkgd", prompt_weight, prompt_vals, preferred_element_type=jnp.float32
    )
    mixed = mixed + jnp.einsum(
        "kgts,skd->tkgd", self_weight, self_vals, preferred_element_type=jnp.float32
    )
    return mixed.reshape(run_len, -1).astype(jnp.bfloat16)


def body(queries, resp_kv, prompt_kv, out_weight, lengths, group_prompt):
    blocks = lengths.shape[0]
    token_count = queries.shape[0]
    run_len = token_count // blocks
    wide_count = lax.axis_size("wide")
    wide_index = lax.axis_index("wide")
    offsets = (wide_index - group_prompt[0]) % wide_count
    query_blocks = queries.reshape(blocks, run_len, queries.shape[1])
    pair_blocks = resp_kv.reshape(2, blocks, run_len, resp_kv.shape[2])
    received = [prompt_kv]
    for offset in range(1, blocks):
        received.append(from_behind(prompt_kv, "wide", offset))
    stacked = jnp.stack(received)

    def one_block(block):
        slot = offsets[block]
        prompt_pair = lax.dynamic_index_in_dim(stacked, slot, 0, keepdims=False)
        block_rows = lax.dynamic_index_in_dim(query_blocks, block, 0, keepdims=False)
        self_pair = lax.dynamic_index_in_dim(pair_blocks, block, 1, keepdims=False)
        block_lengths = lax.dynamic_index_in_dim(lengths, block, 0, keepdims=False)
        return attend_block(block_rows, prompt_pair, self_pair, block_lengths)

    attended = lax.map(one_block, jnp.arange(blocks, dtype=jnp.int32))
    attended = attended.reshape(token_count, -1)
    my_rows = token_count // lax.axis_size("tp")
    everything = lax.psum(
        jnp.dot(attended, out_weight, preferred_element_type=jnp.float32).astype(jnp.bfloat16), "tp"
    ).astype(jnp.float32)
    summed = lax.dynamic_slice_in_dim(everything, lax.axis_index("tp") * my_rows, my_rows, 0)
    return summed.astype(jnp.bfloat16)


def solution(mesh):
    placed = (
        P("wide", "tp"),
        P(None, "wide", "tp"),
        P(None, "wide", "tp"),
        P("tp", None),
        P("wide", None),
        P("wide", None),
    )
    return jax.shard_map(
        body, mesh=mesh, in_specs=placed, out_specs=P(("wide", "tp"), None), check_vma=False
    )
```

profile of v0, /device:TPU:32, one launch (start us, length us, event | category | flops | bytes accessed | tf_op | source)
XLA Modules:
  0.0 323.6 jit_solution(9594626900132623794)
XLA Ops:
  6.5 1.6 collective-permute-start
  8.1 2.9 collective-permute-start.1
  11.0 2.7 collective-permute-start.2
  14.4 42.9 %collective-permute-done = bf16[2,2048,128]{2,1,0:T(8,128)(2,1)S(1)} collective-permute-done((bf16[2,2048,128]{2,1,0:T(8,128)(2,1)}, bf16[2,2048,128]{2,1,0:T(8,128)(2,1)S(1)}, u32[]{:S(2)}, u32[]{:S(2)}) %collective-permute-start) | collective-permute-done | bytes 1048608 | tf_op jit(solution)/shard_map/ppermute | solution.py:14
  57.3 3.3 %pad_maximum_fusion = bf16[4,2,2048,128]{3,2,1,0:T(8,128)(2,1)} fusion(bf16[1,2,2048,128]{3,2,1,0:T(8,128)(2,1)S(1)} %bitcast.115, bf16[1,2,2048,128]{3,2,1,0:T(8,128)(2,1)S(1)} %bitcast.114, bf16[1,2,2048,128]{3,2,1,0:T(8,128)(2,1)S(1)} %bitcast.113, bf16[1,2,2048,128]{3,2,1,0:T(8,128)(2,1)} %bitcast.112), kind=kLoop, calls=%fused_computation.37 | loop fusion | flops 6291456 | bytes 8388608 | tf_op jit(solution)/shard_map/stack | solution.py:70
  60.6 105.8 %while.10 = (s32[]{:T(128)}, bf16[4,128,1024]{2,1,0:T(8,128)(2,1)}, s32[4]{0:T(128)S(1)}, s32[4]{0:T(128)S(1)}, bf16[4,2,2048,128]{3,2,1,0:T(8,128)(2,1)}, /*ind...) while((s32[]{:T(128)}, bf16[4,128,1024]{2,1,0:T(8,128)(2,1)}, ...), condition=%wide.region_7.8_spmd, body=%wide.region_0.7_spmd.sunk | while | flops 1161084288 | bytes 31885136 | solution.py:80
  67.2 5.5 %bitcast_reduce_fusion.2 = (f32[8,128]{1,0:T(8,128)S(1)}, f32[2048,128,8]{1,0,2:T(8,128)}) fusion(bf16[128,8,128]{0,2,1:T(8,128)(2,1)S(1)} %bitcast.108, bf16[4,2,2048,128]{3,2,1,0:T(8,128)(2,1)} %get-tuple-element.169, s32[]{:T(128)S(6)} %select_n.34), kind=kOutput, calls=%fused_computation.1.clone.1 | convolution fusion | flops 541064192 | bytes 9179140 | tf_op jit(solution)/shard_map/while/body/eval_jaxpr/tkgd,skd->kgts/dot_general | solution.py:29
  74.9 4.7 %fusion.43 = f32[8,128]{1,0:T(8,128)S(1)} fusion(f32[2048,128,8]{1,0,2:T(8,128)} %get-tuple-element.137, f32[8,128]{1,0:T(8,128)S(1)} %max.10), kind=kLoop, calls=%fused_computation.4.clone.1 | loop fusion | flops 6290432 | bytes 8396800 | tf_op jit(solution)/shard_map/while/body/eval_jaxpr/reduce_sum | solution.py:44
  79.7 5.5 %fusion.45 = f32[128,8,128]{2,0,1:T(8,128)S(1)} fusion(f32[2048,128,8]{1,0,2:T(8,128)} %get-tuple-element.137, f32[8,128]{1,0:T(8,128)S(1)} %add.58, f32[8,128]{1,0:T(8,128)S(1)} %max.10, bf16[4,2,2048,128]{3,2,1,0:T(8,128)(2,1)} %get-tuple-element.169, s32[]{:T(128)S(6)} %select_n.34, s32[]{:T(128)S(6)} %add.59), kind=kOutput, calls=%fused_computation.5.clone.1 | convolution fusion | flops 545259520 | bytes 9445384 | tf_op jit(solution)/shard_map/while/body/eval_jaxpr/kgts,skd->tkgd/dot_general | solution.py:49
  85.2 1.0 fusion.46
  93.7 5.5 %bitcast_reduce_fusion.2 = (f32[8,128]{1,0:T(8,128)S(1)}, f32[2048,128,8]{1,0,2:T(8,128)}) fusion(bf16[128,8,128]{0,2,1:T(8,128)(2,1)S(1)} %bitcast.108, bf16[4,2,2048,128]{3,2,1,0:T(8,128)(2,1)} %get-tuple-element.169, s32[]{:T(128)S(6)} %select_n.34), kind=kOutput, calls=%fused_computation.1.clone.1 | convolution fusion | flops 541064192 | bytes 9179140 | tf_op jit(solution)/shard_map/while/body/eval_jaxpr/tkgd,skd->kgts/dot_general | solution.py:29
  101.3 4.7 %fusion.43 = f32[8,128]{1,0:T(8,128)S(1)} fusion(f32[2048,128,8]{1,0,2:T(8,128)} %get-tuple-element.137, f32[8,128]{1,0:T(8,128)S(1)} %max.10), kind=kLoop, calls=%fused_computation.4.clone.1 | loop fusion | flops 6290432 | bytes 8396800 | tf_op jit(solution)/shard_map/while/body/eval_jaxpr/reduce_sum | solution.py:44
  106.1 5.5 %fusion.45 = f32[128,8,128]{2,0,1:T(8,128)S(1)} fusion(f32[2048,128,8]{1,0,2:T(8,128)} %get-tuple-element.137, f32[8,128]{1,0:T(8,128)S(1)} %add.58, f32[8,128]{1,0:T(8,128)S(1)} %max.10, bf16[4,2,2048,128]{3,2,1,0:T(8,128)(2,1)} %get-tuple-element.169, s32[]{:T(128)S(6)} %select_n.34, s32[]{:T(128)S(6)} %add.59), kind=kOutput, calls=%fused_computation.5.clone.1 | convolution fusion | flops 545259520 | bytes 9445384 | tf_op jit(solution)/shard_map/while/body/eval_jaxpr/kgts,skd->tkgd/dot_general | solution.py:49
  111.6 1.0 fusion.46
  120.1 5.5 %bitcast_reduce_fusion.2 = (f32[8,128]{1,0:T(8,128)S(1)}, f32[2048,128,8]{1,0,2:T(8,128)}) fusion(bf16[128,8,128]{0,2,1:T(8,128)(2,1)S(1)} %bitcast.108, bf16[4,2,2048,128]{3,2,1,0:T(8,128)(2,1)} %get-tuple-element.169, s32[]{:T(128)S(6)} %select_n.34), kind=kOutput, calls=%fused_computation.1.clone.1 | convolution fusion | flops 541064192 | bytes 9179140 | tf_op jit(solution)/shard_map/while/body/eval_jaxpr/tkgd,skd->kgts/dot_general | solution.py:29
  127.8 4.7 %fusion.43 = f32[8,128]{1,0:T(8,128)S(1)} fusion(f32[2048,128,8]{1,0,2:T(8,128)} %get-tuple-element.137, f32[8,128]{1,0:T(8,128)S(1)} %max.10), kind=kLoop, calls=%fused_computation.4.clone.1 | loop fusion | flops 6290432 | bytes 8396800 | tf_op jit(solution)/shard_map/while/body/eval_jaxpr/reduce_sum | solution.py:44
  132.6 5.5 %fusion.45 = f32[128,8,128]{2,0,1:T(8,128)S(1)} fusion(f32[2048,128,8]{1,0,2:T(8,128)} %get-tuple-element.137, f32[8,128]{1,0:T(8,128)S(1)} %add.58, f32[8,128]{1,0:T(8,128)S(1)} %max.10, bf16[4,2,2048,128]{3,2,1,0:T(8,128)(2,1)} %get-tuple-element.169, s32[]{:T(128)S(6)} %select_n.34, s32[]{:T(128)S(6)} %add.59), kind=kOutput, calls=%fused_computation.5.clone.1 | convolution fusion | flops 545259520 | bytes 9445384 | tf_op jit(solution)/shard_map/while/body/eval_jaxpr/kgts,skd->tkgd/dot_general | solution.py:49
  138.1 1.0 fusion.46
  146.6 5.5 %bitcast_reduce_fusion.2 = (f32[8,128]{1,0:T(8,128)S(1)}, f32[2048,128,8]{1,0,2:T(8,128)}) fusion(bf16[128,8,128]{0,2,1:T(8,128)(2,1)S(1)} %bitcast.108, bf16[4,2,2048,128]{3,2,1,0:T(8,128)(2,1)} %get-tuple-element.169, s32[]{:T(128)S(6)} %select_n.34), kind=kOutput, calls=%fused_computation.1.clone.1 | convolution fusion | flops 541064192 | bytes 9179140 | tf_op jit(solution)/shard_map/while/body/eval_jaxpr/tkgd,skd->kgts/dot_general | solution.py:29
  154.3 4.7 %fusion.43 = f32[8,128]{1,0:T(8,128)S(1)} fusion(f32[2048,128,8]{1,0,2:T(8,128)} %get-tuple-element.137, f32[8,128]{1,0:T(8,128)S(1)} %max.10), kind=kLoop, calls=%fused_computation.4.clone.1 | loop fusion | flops 6290432 | bytes 8396800 | tf_op jit(solution)/shard_map/while/body/eval_jaxpr/reduce_sum | solution.py:44
  159.0 5.5 %fusion.45 = f32[128,8,128]{2,0,1:T(8,128)S(1)} fusion(f32[2048,128,8]{1,0,2:T(8,128)} %get-tuple-element.137, f32[8,128]{1,0:T(8,128)S(1)} %add.58, f32[8,128]{1,0:T(8,128)S(1)} %max.10, bf16[4,2,2048,128]{3,2,1,0:T(8,128)(2,1)} %get-tuple-element.169, s32[]{:T(128)S(6)} %select_n.34, s32[]{:T(128)S(6)} %add.59), kind=kOutput, calls=%fused_computation.5.clone.1 | convolution fusion | flops 545259520 | bytes 9445384 | tf_op jit(solution)/shard_map/while/body/eval_jaxpr/kgts,skd->tkgd/dot_general | solution.py:49
  166.4 10.1 %convolution_convert_fusion = bf16[512,4096]{1,0:T(8,128)(2,1)} fusion(bf16[512,1024]{1,0:T(8,128)(2,1)} %bitcast.117, bf16[1024,4096]{1,0:T(8,128)(2,1)} %param.11), kind=kOutput, calls=%fused_computation.36 | convolution fusion | flops 4297064448 | bytes 13631488 | tf_op jit(solution)/shard_map/dot_general | solution.py:84
  176.6 138.2 %all-reduce.2.cloned.1.call-done = bf16[512,4096]{1,0:T(8,128)(2,1)} async-done(((bf16[512,4096]{1,0:T(8,128)(2,1)}), bf16[512,4096]{1,0:T(8,128)(2,1)}) %all-reduce.2.cloned.1.call-update) | async-done | bytes 4194320 | tf_op jit(solution)/shard_map/psum | solution.py:83
  314.8 1.9 convert_convert_fusion
  (64 shorter events, 23.6 us)
Async XLA Ops:
  6.5 308.3 %all-reduce.2.cloned.1.call-start = ((), (), s32[]{:S(2)}) async-start(), calls=%async_computation | async-start | bytes 8388608 | tf_op jit(solution)/shard_map/psum | solution.py:83
  6.5 50.8 %collective-permute-start = (bf16[2,2048,128]{2,1,0:T(8,128)(2,1)}, bf16[2,2048,128]{2,1,0:T(8,128)(2,1)S(1)}, u32[]{:S(2)}, u32[]{:S(2)}) collective-permute-start(bf16[2,2048,128]{2,1,0:T(8,128)(2,1)} %param.10), channel_id=1, source_target_pairs={{0,8},{8,16},{16,24},{24,32},{32,40},{40,48},{48,56},{56,64},{64,7... | collective-permute-start | bytes 3145736 | tf_op jit(solution)/shard_map/ppermute | solution.py:14
  8.1 49.2 %collective-permute-start.1 = (bf16[2,2048,128]{2,1,0:T(8,128)(2,1)}, bf16[2,2048,128]{2,1,0:T(8,128)(2,1)S(1)}, u32[]{:S(2)}, u32[]{:S(2)}) collective-permute-start(bf16[2,2048,128]{2,1,0:T(8,128)(2,1)} %param.10), channel_id=1, source_target_pairs={{0,16},{8,24},{16,32},{24,40},{32,48},{40,56},{48,64},{56,72},{64,... | collective-permute-start | bytes 3145736 | tf_op jit(solution)/shard_map/ppermute | solution.py:14
  11.0 46.3 %collective-permute-start.2 = (bf16[2,2048,128]{2,1,0:T(8,128)(2,1)}, bf16[2,2048,128]{2,1,0:T(8,128)(2,1)S(1)}, u32[]{:S(2)}, u32[]{:S(2)}) collective-permute-start(bf16[2,2048,128]{2,1,0:T(8,128)(2,1)} %param.10), channel_id=1, source_target_pairs={{0,24},{8,32},{16,40},{24,48},{32,56},{40,64},{48,72},{56,80},{64,... | collective-permute-start | bytes 3145736 | tf_op jit(solution)/shard_map/ppermute | solution.py:14
Sparse Core Ops, SparseCore 0:
  176.7 138.0 all-reduce.1
where the time goes:
time: 325 us; the launch traced here: 324 us
  waiting for transfers between devices  181 us (56%)
  matrix products  62.1 us (19%)
  other arithmetic  26.6 us (8%)
  loops' own time  16.9 us (5%)
  local copies, waits for them, and re-layouts  16.2 us (5%)
  between operations  13.4 us (4%)
  starting transfers between devices  7.18 us (2%)
    psum x1, waiting for transfers between devices, body(): lax.psum(jnp.dot(attended, out_weight, preferred_element_type=jnp.float32...  138 us
    ppermute x3, waiting for transfers between devices, from_behind(): return lax.ppermute(value, axis, pairs)  42.9 us
    dot_general x4, matrix products, attend_block(): jnp.einsum('tkgd,skd->kgts', query_heads, prompt_keys, preferred_element_...  22 us
    dot_general x4, matrix products, attend_block(): jnp.einsum('kgts,skd->tkgd', prompt_weight, prompt_vals, preferred_elemen...  22 us
    reduce_sum x4, other arithmetic, attend_block(): jnp.sum(prompt_exp, axis=-1, keepdims=True)  19 us
    another operation x1, loops' own time, body(): attended = lax.map(one_block, jnp.arange(blocks, dtype=jnp.int32))  16.9 us
    dot_general x1, matrix products, body(): jnp.dot(attended, out_weight, preferred_element_type=jnp.float32)  10.1 us
    ppermute x3, starting transfers between devices, from_behind(): return lax.ppermute(value, axis, pairs)  7.18 us
  transfers between devices with their start and end apart: 4, of which 2 were waited for; matrix products, arithmetic and copies ran while one was open for 0% of the time, Pallas kernels for 0%

commit v1 on v0

v1 whole, which is shorter than its diff:
```python
import functools
import math

import jax
import jax.numpy as jnp
from jax import lax
from jax.experimental import pallas as pl
from jax.experimental.pallas import tpu as pltpu
from jax.sharding import PartitionSpec as P

MESH = pl.DeviceIdType.MESH
HEAD = 128
RUN = 128
HEADS = 8
PROMPT = 2048
KEYS = PROMPT + RUN
D_OUT = 4096
WIDE = 32
CHIPS = 4
HALF = RUN // 2
QUART = D_OUT // CHIPS
CHUNK_HEADS = 4
ROWS = CHUNK_HEADS * RUN
PACK = HEADS * HEAD + 2 * HEAD
EXP_SCALE = math.log2(math.e) / math.sqrt(HEAD)
F32 = jnp.float32
BF16 = jnp.bfloat16


def kernel(
    q_hbm, resp_hbm, prompt_hbm, w_hbm, len_ref, gp_ref,
    out_ref,
    q_buf, resp_buf, keys, vals, w_buf,
    pack_tx, pack_rx, bound_tx, bound_rx, self_vals,
    score0, score1, prob0, prob1, att, part, pair_rx, held, rs_rx, red, home, gather_tx,
    load_sem, pack_send, pack_recv, bound_send, bound_recv,
    pair_send, pair_recv, rs_send, rs_recv, ret_send, ret_recv, gather_send, gather_recv,
):
    wide = lax.axis_index("wide")
    member = lax.axis_index("tp")
    chip = lax.div(member, 2)
    core = lax.rem(member, 2)

    loads = [
        pltpu.make_async_copy(q_hbm, q_buf, load_sem.at[0]),
        pltpu.make_async_copy(resp_hbm, resp_buf, load_sem.at[1]),
        pltpu.make_async_copy(prompt_hbm.at[0], keys, load_sem.at[2]),
        pltpu.make_async_copy(prompt_hbm.at[1], vals.at[:, pl.ds(0, HEAD)], load_sem.at[3]),
        pltpu.make_async_copy(w_hbm, w_buf, load_sem.at[4]),
    ]
    for load in loads:
        load.start()

    def along_wide(steps):
        return {"wide": lax.rem(wide + steps + WIDE, WIDE)}

    def along_chip(steps):
        return {"tp": lax.rem(member + 2 * steps, 2 * CHIPS)}

    sibling = {"tp": member + 1 - 2 * core}

    barrier = pltpu.get_barrier_semaphore()
    partners = [along_wide(s) for s in (-3, -2, -1, 1, 2, 3)] + [along_chip(s) for s in (1, 2, 3)] + [sibling]
    for partner in partners:
        pl.semaphore_signal(barrier, inc=1, device_id=partner, device_id_type=MESH)

    def remote(src, dst, send, recv, device):
        return pltpu.make_async_remote_copy(
            src_ref=src, dst_ref=dst, send_sem=send, recv_sem=recv, device_id=device, device_id_type=MESH
        )

    def slot_at(block):
        return jnp.minimum(lax.rem(wide - gp_ref[0, block] + WIDE, WIDE), 3)

    slot_of = [slot_at(b) for b in range(4)]
    hit = [[1 - jnp.minimum((slot_of[b] - k) * (slot_of[b] - k), 1) for b in range(4)] for k in range(4)]
    block_of = [jnp.minimum(hit[k][1] + 2 * hit[k][2] + 3 * hit[k][3], 3) for k in range(4)]

    vals[:, pl.ds(HEAD, HEAD)] = jnp.ones((PROMPT, HEAD), BF16)
    for s in range(4):
        self_vals[s, :, pl.ds(HEAD, HEAD)] = jnp.ones((RUN, HEAD), BF16)

    loads[0].wait()
    loads[1].wait()
    line = lax.broadcasted_iota(jnp.int32, (8, 128), 0)
    for k in (1, 3, 2, 0):
        target = pack_rx if k == 0 else pack_tx
        bounds = bound_rx if k == 0 else bound_tx
        target[k, :, pl.ds(0, HEADS * HEAD)] = q_buf[block_of[k]]
        target[k, :, pl.ds(HEADS * HEAD, HEAD)] = resp_buf[0, block_of[k]]
        target[k, :, pl.ds((HEADS + 1) * HEAD, HEAD)] = resp_buf[1, block_of[k]]
        first = sum(hit[k][b] * len_ref[b, 0] for b in range(4))
        second = first + sum(hit[k][b] * len_ref[b, 1] for b in range(4))
        third = second + sum(hit[k][b] * len_ref[b, 2] for b in range(4))
        bounds[k] = jnp.where(line == 0, first, jnp.where(line == 1, second, third))

    pl.semaphore_wait(barrier, len(partners))

    packs, bnds = {}, {}
    for k in (1, 2, 3):
        packs[k] = remote(pack_tx.at[k], pack_rx.at[k], pack_send.at[k], pack_recv.at[k], along_wide(-k))
        bnds[k] = remote(bound_tx.at[k], bound_rx.at[k], bound_send.at[k], bound_recv.at[k], along_wide(-k))
    for k in (1, 3):
        bnds[k].start()
        packs[k].start()

    def arrive(s):
        if s:
            bnds[s].wait_recv()
            packs[s].wait_recv()

    def make_scores(s, chunk, score):
        rows = jnp.concatenate(
            [pack_rx[s, :, pl.ds((chunk * CHUNK_HEADS + j) * HEAD, HEAD)] for j in range(CHUNK_HEADS)], axis=0
        )
        dims = (((1,), (1,)), ((), ()))
        score[:, pl.ds(0, PROMPT)] = lax.dot_general(rows, keys[...], dims, preferred_element_type=F32)
        score[:, pl.ds(PROMPT, RUN)] = lax.dot_general(
            rows, pack_rx[s, :, pl.ds(HEADS * HEAD, HEAD)], dims, preferred_element_type=F32
        )

    def make_mask(s):
        at = lax.broadcasted_iota(jnp.int32, (RUN, RUN), 0)
        key_at = lax.broadcasted_iota(jnp.int32, (RUN, RUN), 1)
        begin = jnp.zeros((RUN, RUN), jnp.int32)
        for j in range(3):
            edge = bound_rx[s, pl.ds(j, 1), :]
            begin = jnp.maximum(begin, jnp.where(at >= edge, edge, 0))
        return (key_at >= begin) & (key_at <= at)

    def finish(s, chunk, score, prob):
        mask = make_mask(s)
        for j in range(CHUNK_HEADS):
            here = pl.ds(j * RUN, RUN)
            far = score[here, pl.ds(0, PROMPT)]
            near = jnp.where(mask, score[here, pl.ds(PROMPT, RUN)], -jnp.inf)
            top = jnp.maximum(jnp.max(far, axis=1, keepdims=True), jnp.max(near, axis=1, keepdims=True))
            top = top * EXP_SCALE
            prob[here, pl.ds(0, PROMPT)] = jnp.exp2(far * EXP_SCALE - top).astype(BF16)
            prob[here, pl.ds(PROMPT, RUN)] = jnp.exp2(near * EXP_SCALE - top).astype(BF16)
        mixed = jnp.dot(prob[:, pl.ds(0, PROMPT)], vals[...], preferred_element_type=F32)
        mixed = mixed + jnp.dot(prob[:, pl.ds(PROMPT, RUN)], self_vals[s], preferred_element_type=F32)
        result = (mixed[:, :HEAD] / mixed[:, HEAD:]).astype(BF16)
        for j in range(CHUNK_HEADS):
            att[s, :, pl.ds((chunk * CHUNK_HEADS + j) * HEAD, HEAD)] = result[j * RUN:(j + 1) * RUN]

    def attend(s):
        self_vals[s, :, pl.ds(0, HEAD)] = pack_rx[s, :, pl.ds((HEADS + 1) * HEAD, HEAD)]
        make_scores(s, 0, score0)
        make_scores(s, 1, score1)
        finish(s, 0, score0, prob0)
        finish(s, 1, score1, prob1)

    pairs = {}

    def project(s):
        def columns(i, carry):
            cols = pl.ds(pl.multiple_of(i * QUART, QUART), QUART)
            part[s, :, cols] = jnp.dot(att[s], w_buf[:, cols], preferred_element_type=F32).astype(BF16)
            return carry

        lax.fori_loop(0, D_OUT // QUART, columns, 0)
        theirs = pl.ds(pl.multiple_of((1 - core) * HALF, HALF), HALF)
        pairs[s] = remote(part.at[s, theirs], pair_rx.at[s], pair_send.at[s], pair_recv.at[s], sibling)
        pairs[s].start()

    rs = {}

    def combine(s):
        pairs[s].wait_recv()
        mine = pl.ds(pl.multiple_of(core * HALF, HALF), HALF)
        held[s] = (part[s, mine, :].astype(F32) + pair_rx[s].astype(F32)).astype(BF16)
        for j in (1, 3, 2):
            there = lax.rem(chip + j, CHIPS)
            cols = pl.ds(pl.multiple_of(there * QUART, QUART), QUART)
            rs[s, j] = remote(
                held.at[s, :, cols], rs_rx.at[s, j], rs_send.at[s, j], rs_recv.at[s, j], along_chip(j)
            )
            rs[s, j].start()

    returns = {}

    def reduce(s):
        for j in (1, 3, 2):
            rs[s, j].wait_recv()
        cols = pl.ds(pl.multiple_of(chip * QUART, QUART), QUART)
        total = held[s, :, cols].astype(F32)
        for j in (1, 2, 3):
            total = total + rs_rx[s, j].astype(F32)
        if s == 0:
            home[0] = total.astype(BF16)
        else:
            red[s] = total.astype(BF16)
            returns[s] = remote(red.at[s], home.at[s], ret_send.at[s], ret_recv.at[s], along_wide(s))
            returns[s].start()

    loads[2].wait()
    loads[3].wait()
    attend(0)
    for k in (1, 3):
        bnds[k].wait_send()
        packs[k].wait_send()
    bnds[2].start()
    packs[2].start()
    loads[4].wait()
    project(0)
    arrive(1)
    attend(1)
    combine(0)
    project(1)
    arrive(3)
    attend(3)
    combine(1)
    project(3)
    reduce(0)
    reduce(1)
    arrive(2)
    attend(2)
    combine(3)
    project(2)
    reduce(3)
    combine(2)
    reduce(2)

    for k in (1, 2, 3):
        returns[k].wait_recv()

    mine = pl.ds(pl.multiple_of(chip * QUART, QUART), QUART)
    gathers = []
    for j in (1, 3, 2):
        there = lax.rem(chip + j, CHIPS)
        gather_tx[j] = home[slot_at(there)]
        copy = remote(gather_tx.at[j], out_ref.at[:, mine], gather_send.at[j], gather_recv.at[j], along_chip(j))
        copy.start()
        gathers.append(copy)
    out_ref[:, mine] = home[slot_at(chip)]

    bnds[2].wait_send()
    packs[2].wait_send()
    for s in range(4):
        pairs[s].wait_send()
        for j in (1, 2, 3):
            rs[s, j].wait_send()
        if s:
            returns[s].wait_send()
    for copy in gathers:
        copy.wait_send()
        copy.wait_recv()


def body(queries, resp_kv, prompt_kv, out_weight, lengths, group_prompt):
    queries = queries.reshape(4, RUN, HEADS * HEAD)
    resp_kv = resp_kv.reshape(2, 4, RUN, HEAD)
    hbm = pl.BlockSpec(memory_space=pl.ANY)
    smem = pl.BlockSpec(memory_space=pltpu.SMEM)
    dma = pltpu.SemaphoreType.DMA
    return pl.pallas_call(
        kernel,
        out_shape=jax.ShapeDtypeStruct((HALF, D_OUT), BF16),
        in_specs=[hbm, hbm, hbm, hbm, smem, smem],
        out_specs=pl.BlockSpec(memory_space=pltpu.VMEM),
        scratch_shapes=[
            pltpu.VMEM((4, RUN, HEADS * HEAD), BF16),
            pltpu.VMEM((2, 4, RUN, HEAD), BF16),
            pltpu.VMEM((PROMPT, HEAD), BF16),
            pltpu.VMEM((PROMPT, 2 * HEAD), BF16),
            pltpu.VMEM((HEADS * HEAD, D_OUT), BF16),
            pltpu.VMEM((4, RUN, PACK), BF16),
            pltpu.VMEM((4, RUN, PACK), BF16),
            pltpu.VMEM((4, 8, 128), jnp.int32),
            pltpu.VMEM((4, 8, 128), jnp.int32),
            pltpu.VMEM((4, RUN, 2 * HEAD), BF16),
            pltpu.VMEM((ROWS, KEYS), F32),
            pltpu.VMEM((ROWS, KEYS), F32),
            pltpu.VMEM((ROWS, KEYS), BF16),
            pltpu.VMEM((ROWS, KEYS), BF16),
            pltpu.VMEM((4, RUN, HEADS * HEAD), BF16),
            pltpu.VMEM((4, RUN, D_OUT), BF16),
            pltpu.VMEM((4, HALF, D_OUT), BF16),
            pltpu.VMEM((4, HALF, D_OUT), BF16),
            pltpu.VMEM((4, 4, HALF, QUART), BF16),
            pltpu.VMEM((4, HALF, QUART), BF16),
            pltpu.VMEM((4, HALF, QUART), BF16),
            pltpu.VMEM((4, HALF, QUART), BF16),
            dma((5,)),
            dma((4,)), dma((4,)), dma((4,)), dma((4,)),
            dma((4,)), dma((4,)), dma((4, 4)), dma((4, 4)), dma((4,)), dma((4,)), dma((4,)), dma((4,)),
        ],
        compiler_params=pltpu.CompilerParams(
            collective_id=1, has_side_effects=True, vmem_limit_bytes=60 * 1024 * 1024
        ),
        cost_estimate=pl.CostEstimate(flops=9 * 10**9, bytes_accessed=12 * 2**20, transcendentals=9 * 10**6),
    )(queries, resp_kv, prompt_kv, out_weight, lengths, group_prompt)


def solution(mesh):
    placed = (
        P("wide", "tp"),
        P(None, "wide", "tp"),
        P(None, "wide", "tp"),
        P("tp", None),
        P("wide", None),
        P("wide", None),
    )
    return jax.shard_map(
        body, mesh=mesh, in_specs=placed, out_specs=P(("wide", "tp"), None), check_vma=False
    )
```

time: 325 us -> 72.1 us (0.22)
  waiting for transfers between devices: 181 us -> 0 us
  Pallas kernels: 0 us -> 70.1 us
  matrix products: 62.1 us -> 0 us
  other arithmetic: 26.6 us -> 0 us
  loops' own time: 16.9 us -> 0 us
  local copies, waits for them, and re-layouts: 16.2 us -> 1.87 us
  between operations: 13.4 us -> 0.01 us
  starting transfers between devices: 7.18 us -> 0 us
    psum x1 -> x0, waiting for transfers between devices: 138 us -> none  [body(): lax.psum(jnp.dot(attended, out_weight, preferred_element_type=jnp.float32...]
    pallas_call x0 -> x1, Pallas kernels: none -> 70.1 us  [body(): pl.pallas_call(kernel, out_shape=jax.ShapeDtypeStruct((HALF, D_OUT), BF16...]
    dot_general x17 -> x0, matrix products: 62.1 us -> none  [the longest x4 22 us: attend_block(): jnp.einsum('tkgd,skd->kgts', query_heads, prompt_keys, preferred_element_...]
    ppermute x3 -> x0, waiting for transfers between devices: 42.9 us -> none  [from_behind(): return lax.ppermute(value, axis, pairs)]
    reduce_sum x12 -> x0, other arithmetic: 19.7 us -> none  [the longest x4 19 us: attend_block(): jnp.sum(prompt_exp, axis=-1, keepdims=True)]
    another operation x1 -> x0, loops' own time: 16.9 us -> none  [body(): attended = lax.map(one_block, jnp.arange(blocks, dtype=jnp.int32))]
    dynamic_slice x16 -> x0, local copies, waits for them, and re-layouts: 9.9 us -> none  [the longest x8 4.57 us: one_block(): lax.dynamic_index_in_dim(query_blocks, block, 0, keepdims=False)]
    ppermute x3 -> x0, starting transfers between devices: 7.18 us -> none  [from_behind(): return lax.ppermute(value, axis, pairs)]
  transfers between devices with their start and end apart: 4 -> 0, of which waited for: 2 -> 0; matrix products, arithmetic and copies ran while one was open for 0% -> 0% of each run, Pallas kernels for 0% -> 0%
where the time goes in v1:
time: 72.1 us; the launch traced here: 72 us
  Pallas kernels  70.1 us (97%)
  local copies, waits for them, and re-layouts  1.87 us (3%)
    pallas_call x1, Pallas kernels, body(): pl.pallas_call(kernel, out_shape=jax.ShapeDtypeStruct((HALF, D_OUT), BF16...  70.1 us
    unnamed x1, local copies, waits for them, and re-layouts  1.87 us

profile of v1, /device:TPU:32, one launch (start us, length us, event | category | flops | bytes accessed | tf_op | source)
XLA Modules:
  0.0 72.0 jit_solution(15009009923812170243)
XLA Ops:
  0.0 70.1 %shard_map.64 = bf16[64,4096]{1,0:T(8,128)(2,1)} custom-call(bf16[4,128,1024]{2,1,0:T(8,128)(2,1)} %bitcast.2, bf16[2,4,128,128]{3,2,1,0:T(8,128)(2,1)} %bitcast.3, bf16[2,2048,128]{2,1,0:T(8,128)(2,1)} %prompt_hbm.1, bf16[1024,4096]{1,0:T(8,128)(2,1)} %w_hbm.1, s32[4,4]{1,0:T(4,128)} %len_ref.1, s32[1,4]{1,0:T(1,128)} %gp_ref.1), custom_call_target="tpu_custom_call" | custom-call | flops 8999999488 | bytes 12582912 | tf_op jit(solution)/shard_map/pallas_call | solution.py:257
  70.1 1.9 %copy.8 = bf16[64,4096]{1,0:T(8,128)(2,1)} copy(bf16[64,4096]{1,0:T(8,128)(2,1)} %shard_map.64) | data formatting | bytes 1048576

commit v2 on v1

--- a/solution.py
+++ b/solution.py
@@ -32,7 +32,7 @@
     out_ref,
     q_buf, resp_buf, keys, vals, w_buf,
     pack_tx, pack_rx, bound_tx, bound_rx, self_vals,
-    score0, score1, prob0, prob1, att, part, pair_rx, held, rs_rx, red, home, gather_tx,
+    score0, score1, prob0, prob1, att, part, pair_rx, held, relay_rx, relay_tx, sum_rx, red, home, gather_tx,
     load_sem, pack_send, pack_recv, bound_send, bound_recv,
     pair_send, pair_recv, rs_send, rs_recv, ret_send, ret_recv, gather_send, gather_recv,
 ):
@@ -48,7 +48,7 @@
         pltpu.make_async_copy(prompt_hbm.at[1], vals.at[:, pl.ds(0, HEAD)], load_sem.at[3]),
         pltpu.make_async_copy(w_hbm, w_buf, load_sem.at[4]),
     ]
-    for load in loads:
+    for load in loads[:4]:
         load.start()
 
     def along_wide(steps):
@@ -82,8 +82,10 @@
 
     loads[0].wait()
     loads[1].wait()
+    loads[4].start()
     line = lax.broadcasted_iota(jnp.int32, (8, 128), 0)
-    for k in (1, 3, 2, 0):
+
+    def stage(k):
         target = pack_rx if k == 0 else pack_tx
         bounds = bound_rx if k == 0 else bound_tx
         target[k, :, pl.ds(0, HEADS * HEAD)] = q_buf[block_of[k]]
@@ -94,20 +96,26 @@
         third = second + sum(hit[k][b] * len_ref[b, 2] for b in range(4))
         bounds[k] = jnp.where(line == 0, first, jnp.where(line == 1, second, third))
 
+    bnds = {
+        k: remote(bound_tx.at[k], bound_rx.at[k], bound_send.at[k], bound_recv.at[k], along_wide(-k)) for k in (1, 2, 3)
+    }
+    packs = {
+        k: remote(pack_tx.at[k], pack_rx.at[k], pack_send.at[k], pack_recv.at[k], along_wide(-k)) for k in (1, 2, 3)
+    }
+
+    stage(1)
     pl.semaphore_wait(barrier, len(partners))
 
-    packs, bnds = {}, {}
-    for k in (1, 2, 3):
-        packs[k] = remote(pack_tx.at[k], pack_rx.at[k], pack_send.at[k], pack_recv.at[k], along_wide(-k))
-        bnds[k] = remote(bound_tx.at[k], bound_rx.at[k], bound_send.at[k], bound_recv.at[k], along_wide(-k))
-    for k in (1, 3):
-        bnds[k].start()
-        packs[k].start()
+    packs[1].start()
+    stage(3)
+    packs[3].start()
+    bnds[1].start()
+    bnds[3].start()
+    stage(0)
 
     def arrive(s):
-        if s:
-            bnds[s].wait_recv()
-            packs[s].wait_recv()
+        bnds[s].wait_recv()
+        packs[s].wait_recv()
 
     def make_scores(s, chunk, score):
         rows = jnp.concatenate(
@@ -151,96 +159,116 @@
         finish(s, 0, score0, prob0)
         finish(s, 1, score1, prob1)
 
-    pairs = {}
-
-    def project(s):
-        def columns(i, carry):
-            cols = pl.ds(pl.multiple_of(i * QUART, QUART), QUART)
-            part[s, :, cols] = jnp.dot(att[s], w_buf[:, cols], preferred_element_type=F32).astype(BF16)
-            return carry
-
-        lax.fori_loop(0, D_OUT // QUART, columns, 0)
-        theirs = pl.ds(pl.multiple_of((1 - core) * HALF, HALF), HALF)
-        pairs[s] = remote(part.at[s, theirs], pair_rx.at[s], pair_send.at[s], pair_recv.at[s], sibling)
-        pairs[s].start()
-
-    rs = {}
-
-    def combine(s):
-        pairs[s].wait_recv()
-        mine = pl.ds(pl.multiple_of(core * HALF, HALF), HALF)
-        held[s] = (part[s, mine, :].astype(F32) + pair_rx[s].astype(F32)).astype(BF16)
-        for j in (1, 3, 2):
-            there = lax.rem(chip + j, CHIPS)
-            cols = pl.ds(pl.multiple_of(there * QUART, QUART), QUART)
-            rs[s, j] = remote(
-                held.at[s, :, cols], rs_rx.at[s, j], rs_send.at[s, j], rs_recv.at[s, j], along_chip(j)
-            )
-            rs[s, j].start()
+    ahead, behind = lax.rem(chip + 1, CHIPS), lax.rem(chip + CHIPS - 1, CHIPS)
+    across = lax.rem(chip + 2, CHIPS)
+    mine = pl.ds(pl.multiple_of(core * HALF, HALF), HALF)
+    theirs = pl.ds(pl.multiple_of((1 - core) * HALF, HALF), HALF)
+
+    def quarter(there):
+        return pl.ds(pl.multiple_of(there * QUART, QUART), QUART)
+
+    def eighth(there, half):
+        return pl.ds(pl.multiple_of(there * QUART + half * (QUART // 2), QUART // 2), QUART // 2)
+
+    pairs, rs = {}, {}
+
+    def project(s, i, there):
+        cols = quarter(there)
+        part[s, :, cols] = jnp.dot(att[s], w_buf[:, cols], preferred_element_type=F32).astype(BF16)
+        pairs[s, i] = remote(
+            part.at[s, theirs, cols], pair_rx.at[s, :, cols], pair_send.at[s, i], pair_recv.at[s, i], sibling
+        )
+        pairs[s, i].start()
+
+    def combine(s, i, there):
+        pairs[s, i].wait_recv()
+        cols = quarter(there)
+        held[s, :, cols] = (part[s, mine, cols].astype(F32) + pair_rx[s, :, cols].astype(F32)).astype(BF16)
+
+    def rs_start(s, i, src, dst, steps):
+        rs[s, i] = remote(src, dst, rs_send.at[s, i], rs_recv.at[s, i], along_chip(steps))
+        rs[s, i].start()
+
+    def spread(s):
+        order = (across, ahead, behind, chip)
+        for i, there in enumerate(order):
+            project(s, i, there)
+        for i, there in enumerate(order):
+            combine(s, i, there)
+            if i == 0:
+                rs_start(s, 0, held.at[s, :, eighth(across, 0)], relay_rx.at[s, 0], 1)
+                rs_start(s, 1, held.at[s, :, eighth(across, 1)], relay_rx.at[s, 1], 3)
+        rs_start(s, 2, held.at[s, :, eighth(ahead, 1)], sum_rx.at[s, 0], 1)
+        rs_start(s, 3, held.at[s, :, eighth(behind, 0)], sum_rx.at[s, 1], 3)
+
+    def relay(s):
+        for i, (there, steps) in enumerate(((ahead, 1), (behind, 3))):
+            rs[s, i].wait_recv()
+            own = held[s, :, eighth(there, i)].astype(F32)
+            relay_tx[s, i] = (own + relay_rx[s, i].astype(F32)).astype(BF16)
+            rs_start(s, 4 + i, relay_tx.at[s, i], sum_rx.at[s, 2 + i], steps)
 
     returns = {}
 
     def reduce(s):
-        for j in (1, 3, 2):
-            rs[s, j].wait_recv()
-        cols = pl.ds(pl.multiple_of(chip * QUART, QUART), QUART)
-        total = held[s, :, cols].astype(F32)
-        for j in (1, 2, 3):
-            total = total + rs_rx[s, j].astype(F32)
-        if s == 0:
-            home[0] = total.astype(BF16)
-        else:
-            red[s] = total.astype(BF16)
+        for i in (2, 3, 4, 5):
+            rs[s, i].wait_recv()
+        target = home if s == 0 else red
+        for half in (0, 1):
+            total = held[s, :, eighth(chip, half)].astype(F32)
+            total = total + sum_rx[s, 1 - half].astype(F32) + sum_rx[s, 2 + half].astype(F32)
+            target[s, :, pl.ds(half * (QUART // 2), QUART // 2)] = total.astype(BF16)
+        if s:
             returns[s] = remote(red.at[s], home.at[s], ret_send.at[s], ret_recv.at[s], along_wide(s))
             returns[s].start()
 
     loads[2].wait()
     loads[3].wait()
     attend(0)
-    for k in (1, 3):
-        bnds[k].wait_send()
-        packs[k].wait_send()
+    stage(2)
+    loads[4].wait()
+    spread(0)
+    packs[2].start()
     bnds[2].start()
-    packs[2].start()
-    loads[4].wait()
-    project(0)
+    relay(0)
+    arrive(3)
+    attend(3)
+    spread(3)
+    reduce(0)
     arrive(1)
     attend(1)
-    combine(0)
-    project(1)
-    arrive(3)
-    attend(3)
-    combine(1)
-    project(3)
-    reduce(0)
-    reduce(1)
+    relay(3)
+    spread(1)
+    reduce(3)
     arrive(2)
     attend(2)
-    combine(3)
-    project(2)
-    reduce(3)
-    combine(2)
+    relay(1)
+    spread(2)
+    reduce(1)
+    relay(2)
     reduce(2)
 
     for k in (1, 2, 3):
         returns[k].wait_recv()
 
-    mine = pl.ds(pl.multiple_of(chip * QUART, QUART), QUART)
+    here = quarter(chip)
     gathers = []
     for j in (1, 3, 2):
         there = lax.rem(chip + j, CHIPS)
         gather_tx[j] = home[slot_at(there)]
-        copy = remote(gather_tx.at[j], out_ref.at[:, mine], gather_send.at[j], gather_recv.at[j], along_chip(j))
+        copy = remote(gather_tx.at[j], out_ref.at[:, here], gather_send.at[j], gather_recv.at[j], along_chip(j))
         copy.start()
         gathers.append(copy)
-    out_ref[:, mine] = home[slot_at(chip)]
-
-    bnds[2].wait_send()
-    packs[2].wait_send()
+    out_ref[:, here] = home[slot_at(chip)]
+
+    for k in (1, 2, 3):
+        bnds[k].wait_send()
+        packs[k].wait_send()
     for s in range(4):
-        pairs[s].wait_send()
-        for j in (1, 2, 3):
-            rs[s, j].wait_send()
+        for i in range(4):
+            pairs[s, i].wait_send()
+        for i in range(6):
+            rs[s, i].wait_send()
         if s:
             returns[s].wait_send()
     for copy in gathers:
@@ -278,13 +306,15 @@
             pltpu.VMEM((4, RUN, D_OUT), BF16),
             pltpu.VMEM((4, HALF, D_OUT), BF16),
             pltpu.VMEM((4, HALF, D_OUT), BF16),
-            pltpu.VMEM((4, 4, HALF, QUART), BF16),
+            pltpu.VMEM((4, 2, HALF, QUART // 2), BF16),
+            pltpu.VMEM((4, 2, HALF, QUART // 2), BF16),
+            pltpu.VMEM((4, 4, HALF, QUART // 2), BF16),
             pltpu.VMEM((4, HALF, QUART), BF16),
             pltpu.VMEM((4, HALF, QUART), BF16),
             pltpu.VMEM((4, HALF, QUART), BF16),
             dma((5,)),
             dma((4,)), dma((4,)), dma((4,)), dma((4,)),
-            dma((4,)), dma((4,)), dma((4, 4)), dma((4, 4)), dma((4,)), dma((4,)), dma((4,)), dma((4,)),
+            dma((4, 4)), dma((4, 4)), dma((4, 6)), dma((4, 6)), dma((4,)), dma((4,)), dma((4,)), dma((4,)),
         ],
         compiler_params=pltpu.CompilerParams(
             collective_id=1, has_side_effects=True, vmem_limit_bytes=60 * 1024 * 1024

time: 72.1 us -> 63.1 us (0.88)
  the two profiles are of different devices: /device:TPU:32 before, /device:TPU:120 now
where the time goes in v2:
time: 63.1 us; the launch traced here: 62.9 us
  Pallas kernels  61 us (97%)
  local copies, waits for them, and re-layouts  1.87 us (3%)
    pallas_call x1, Pallas kernels, body(): pl.pallas_call(kernel, out_shape=jax.ShapeDtypeStruct((HALF, D_OUT), BF16...  61 us
    unnamed x1, local copies, waits for them, and re-layouts  1.87 us

profile of v2, /device:TPU:120, one launch (start us, length us, event | category | flops | bytes accessed | tf_op | source)
XLA Modules:
  0.0 62.9 jit_solution(3731540577171573958)
XLA Ops:
  0.0 61.0 %shard_map.64 = bf16[64,4096]{1,0:T(8,128)(2,1)} custom-call(bf16[4,128,1024]{2,1,0:T(8,128)(2,1)} %bitcast.2, bf16[2,4,128,128]{3,2,1,0:T(8,128)(2,1)} %bitcast.3, bf16[2,2048,128]{2,1,0:T(8,128)(2,1)} %prompt_hbm.1, bf16[1024,4096]{1,0:T(8,128)(2,1)} %w_hbm.1, s32[4,4]{1,0:T(4,128)} %len_ref.1, s32[1,4]{1,0:T(1,128)} %gp_ref.1), custom_call_target="tpu_custom_call" | custom-call | flops 8999999488 | bytes 12582912 | tf_op jit(solution)/shard_map/pallas_call | solution.py:285
  61.0 1.9 %copy.8 = bf16[64,4096]{1,0:T(8,128)(2,1)} copy(bf16[64,4096]{1,0:T(8,128)(2,1)} %shard_map.64) | data formatting | bytes 1048576

commit v3 on v2

--- a/solution.py
+++ b/solution.py
@@ -19,6 +19,8 @@
 CHIPS = 4
 HALF = RUN // 2
 QUART = D_OUT // CHIPS
+MID = QUART // 2
+LAST = 3
 CHUNK_HEADS = 4
 ROWS = CHUNK_HEADS * RUN
 PACK = HEADS * HEAD + 2 * HEAD
@@ -32,7 +34,7 @@
     out_ref,
     q_buf, resp_buf, keys, vals, w_buf,
     pack_tx, pack_rx, bound_tx, bound_rx, self_vals,
-    score0, score1, prob0, prob1, att, part, pair_rx, held, relay_rx, relay_tx, sum_rx, red, home, gather_tx,
+    score0, score1, prob0, prob1, att, part, pair_rx, held, relay_rx, relay_tx, sum_rx, red, home_low, home_high, gather_tx,
     load_sem, pack_send, pack_recv, bound_send, bound_recv,
     pair_send, pair_recv, rs_send, rs_recv, ret_send, ret_recv, gather_send, gather_recv,
 ):
@@ -113,18 +115,24 @@
     bnds[3].start()
     stage(0)
 
+    column = lax.rem(wide, CHIPS)
+    differs = 1 - jnp.minimum((column - 1) * (column - 1), 1)
+    turn = (0, 3 - 2 * differs, 1 + differs, 2 + differs)
+
     def arrive(s):
-        bnds[s].wait_recv()
-        packs[s].wait_recv()
+        k = turn[s]
+        back = along_wide(-k)
+        remote(bound_tx.at[k], bound_rx.at[k], bound_send.at[k], bound_recv.at[k], back).wait_recv()
+        remote(pack_tx.at[k], pack_rx.at[k], pack_send.at[k], pack_recv.at[k], back).wait_recv()
 
     def make_scores(s, chunk, score):
         rows = jnp.concatenate(
-            [pack_rx[s, :, pl.ds((chunk * CHUNK_HEADS + j) * HEAD, HEAD)] for j in range(CHUNK_HEADS)], axis=0
+            [pack_rx[turn[s], :, pl.ds((chunk * CHUNK_HEADS + j) * HEAD, HEAD)] for j in range(CHUNK_HEADS)], axis=0
         )
         dims = (((1,), (1,)), ((), ()))
         score[:, pl.ds(0, PROMPT)] = lax.dot_general(rows, keys[...], dims, preferred_element_type=F32)
         score[:, pl.ds(PROMPT, RUN)] = lax.dot_general(
-            rows, pack_rx[s, :, pl.ds(HEADS * HEAD, HEAD)], dims, preferred_element_type=F32
+            rows, pack_rx[turn[s], :, pl.ds(HEADS * HEAD, HEAD)], dims, preferred_element_type=F32
         )
 
     def make_mask(s):
@@ -132,7 +140,7 @@
         key_at = lax.broadcasted_iota(jnp.int32, (RUN, RUN), 1)
         begin = jnp.zeros((RUN, RUN), jnp.int32)
         for j in range(3):
-            edge = bound_rx[s, pl.ds(j, 1), :]
+            edge = bound_rx[turn[s], pl.ds(j, 1), :]
             begin = jnp.maximum(begin, jnp.where(at >= edge, edge, 0))
         return (key_at >= begin) & (key_at <= at)
 
@@ -153,7 +161,7 @@
             att[s, :, pl.ds((chunk * CHUNK_HEADS + j) * HEAD, HEAD)] = result[j * RUN:(j + 1) * RUN]
 
     def attend(s):
-        self_vals[s, :, pl.ds(0, HEAD)] = pack_rx[s, :, pl.ds((HEADS + 1) * HEAD, HEAD)]
+        self_vals[s, :, pl.ds(0, HEAD)] = pack_rx[turn[s], :, pl.ds((HEADS + 1) * HEAD, HEAD)]
         make_scores(s, 0, score0)
         make_scores(s, 1, score1)
         finish(s, 0, score0, prob0)
@@ -164,113 +172,156 @@
     mine = pl.ds(pl.multiple_of(core * HALF, HALF), HALF)
     theirs = pl.ds(pl.multiple_of((1 - core) * HALF, HALF), HALF)
 
-    def quarter(there):
-        return pl.ds(pl.multiple_of(there * QUART, QUART), QUART)
-
-    def eighth(there, half):
-        return pl.ds(pl.multiple_of(there * QUART + half * (QUART // 2), QUART // 2), QUART // 2)
-
-    pairs, rs = {}, {}
-
-    def project(s, i, there):
-        cols = quarter(there)
-        part[s, :, cols] = jnp.dot(att[s], w_buf[:, cols], preferred_element_type=F32).astype(BF16)
-        pairs[s, i] = remote(
-            part.at[s, theirs, cols], pair_rx.at[s, :, cols], pair_send.at[s, i], pair_recv.at[s, i], sibling
-        )
-        pairs[s, i].start()
-
-    def combine(s, i, there):
-        pairs[s, i].wait_recv()
-        cols = quarter(there)
+    def span(there, start, width):
+        return pl.ds(pl.multiple_of(there * QUART + start, HEAD), width)
+
+    def piece(s, p):
+        return (p * MID, MID) if s == LAST else (0, QUART)
+
+    pairs, rs, returns = {}, {}, {}
+    order = (across, ahead, behind, chip)
+
+    def project(s, p):
+        start, width = piece(s, p)
+        for i, there in enumerate(order):
+            cols = span(there, start, width)
+            part[s, :, cols] = jnp.dot(att[s], w_buf[:, cols], preferred_element_type=F32).astype(BF16)
+            pairs[s, p, i] = remote(
+                part.at[s, theirs, cols], pair_rx.at[s, :, cols], pair_send.at[s, p, i], pair_recv.at[s, p, i], sibling
+            )
+            pairs[s, p, i].start()
+
+    def rs_start(s, p, i, src, dst, steps):
+        rs[s, p, i] = remote(src, dst, rs_send.at[s, p, i], rs_recv.at[s, p, i], along_chip(steps))
+        rs[s, p, i].start()
+
+    def portion(s, p, there, half):
+        start, width = piece(s, p)
+        return span(there, start + half * (width // 2), width // 2)
+
+    def slots(s, p):
+        width = piece(s, p)[1] // 2
+        return pl.ds(p * width, width)
+
+    def combine(s, p, i):
+        pairs[s, p, i].wait_recv()
+        cols = span(order[i], *piece(s, p))
         held[s, :, cols] = (part[s, mine, cols].astype(F32) + pair_rx[s, :, cols].astype(F32)).astype(BF16)
 
-    def rs_start(s, i, src, dst, steps):
-        rs[s, i] = remote(src, dst, rs_send.at[s, i], rs_recv.at[s, i], along_chip(steps))
-        rs[s, i].start()
-
-    def spread(s):
-        order = (across, ahead, behind, chip)
-        for i, there in enumerate(order):
-            project(s, i, there)
-        for i, there in enumerate(order):
-            combine(s, i, there)
-            if i == 0:
-                rs_start(s, 0, held.at[s, :, eighth(across, 0)], relay_rx.at[s, 0], 1)
-                rs_start(s, 1, held.at[s, :, eighth(across, 1)], relay_rx.at[s, 1], 3)
-        rs_start(s, 2, held.at[s, :, eighth(ahead, 1)], sum_rx.at[s, 0], 1)
-        rs_start(s, 3, held.at[s, :, eighth(behind, 0)], sum_rx.at[s, 1], 3)
-
-    def relay(s):
-        for i, (there, steps) in enumerate(((ahead, 1), (behind, 3))):
-            rs[s, i].wait_recv()
-            own = held[s, :, eighth(there, i)].astype(F32)
-            relay_tx[s, i] = (own + relay_rx[s, i].astype(F32)).astype(BF16)
-            rs_start(s, 4 + i, relay_tx.at[s, i], sum_rx.at[s, 2 + i], steps)
-
-    returns = {}
-
-    def reduce(s):
+    def combine_far(s, p):
+        combine(s, p, 0)
+        there = slots(s, p)
+        rs_start(s, p, 0, held.at[s, :, portion(s, p, across, 0)], relay_rx.at[s, 0, :, there], 1)
+        rs_start(s, p, 1, held.at[s, :, portion(s, p, across, 1)], relay_rx.at[s, 1, :, there], 3)
+
+    def combine_near(s, p):
+        for i in (1, 2, 3):
+            combine(s, p, i)
+        there = slots(s, p)
+        rs_start(s, p, 2, held.at[s, :, portion(s, p, ahead, 1)], sum_rx.at[s, 0, :, there], 1)
+        rs_start(s, p, 3, held.at[s, :, portion(s, p, behind, 0)], sum_rx.at[s, 1, :, there], 3)
+
+    def relay(s, p):
+        there = slots(s, p)
+        for i, (goal, steps) in enumerate(((ahead, 1), (behind, 3))):
+            rs[s, p, i].wait_recv()
+            own = held[s, :, portion(s, p, goal, i)].astype(F32)
+            relay_tx[s, i, :, there] = (own + relay_rx[s, i, :, there].astype(F32)).astype(BF16)
+            rs_start(s, p, 4 + i, relay_tx.at[s, i, :, there], sum_rx.at[s, 2 + i, :, there], steps)
+
+    homes = (home_low, home_high)
+
+    def reduce(s, p):
         for i in (2, 3, 4, 5):
-            rs[s, i].wait_recv()
-        target = home if s == 0 else red
+            rs[s, p, i].wait_recv()
+        there = slots(s, p)
+        start, width = piece(s, p)
         for half in (0, 1):
-            total = held[s, :, eighth(chip, half)].astype(F32)
-            total = total + sum_rx[s, 1 - half].astype(F32) + sum_rx[s, 2 + half].astype(F32)
-            target[s, :, pl.ds(half * (QUART // 2), QUART // 2)] = total.astype(BF16)
+            total = held[s, :, portion(s, p, chip, half)].astype(F32)
+            total = total + sum_rx[s, 1 - half, :, there].astype(F32) + sum_rx[s, 2 + half, :, there].astype(F32)
+            at = start + half * (width // 2)
+            if s == 0:
+                homes[half][s] = total.astype(BF16)
+            else:
+                red[s, :, pl.ds(at, width // 2)] = total.astype(BF16)
         if s:
-            returns[s] = remote(red.at[s], home.at[s], ret_send.at[s], ret_recv.at[s], along_wide(s))
-            returns[s].start()
+            for h in ((p,) if s == LAST else (0, 1)):
+                k = turn[s]
+                returns[s, h] = remote(
+                    red.at[s, :, pl.ds(h * MID, MID)], homes[h].at[k], ret_send.at[s, h], ret_recv.at[k, h], along_wide(k)
+                )
+                returns[s, h].start()
 
     loads[2].wait()
     loads[3].wait()
     attend(0)
     stage(2)
     loads[4].wait()
-    spread(0)
-    packs[2].start()
-    bnds[2].start()
-    relay(0)
+    project(0, 0)
+    combine_far(0, 0)
+    combine_near(0, 0)
+
+    @pl.when(column != 0)
+    def _():
+        packs[2].start()
+        bnds[2].start()
+
+    relay(0, 0)
+    arrive(1)
+    attend(1)
+
+    @pl.when(column == 0)
+    def _():
+        packs[2].start()
+        bnds[2].start()
+
+    project(1, 0)
+    combine_far(1, 0)
+    combine_near(1, 0)
+    reduce(0, 0)
+    arrive(2)
+    attend(2)
+    relay(1, 0)
+    project(2, 0)
+    combine_far(2, 0)
+    combine_near(2, 0)
+    reduce(1, 0)
     arrive(3)
     attend(3)
-    spread(3)
-    reduce(0)
-    arrive(1)
-    attend(1)
-    relay(3)
-    spread(1)
-    reduce(3)
-    arrive(2)
-    attend(2)
-    relay(1)
-    spread(2)
-    reduce(1)
-    relay(2)
-    reduce(2)
-
-    for k in (1, 2, 3):
-        returns[k].wait_recv()
-
-    here = quarter(chip)
+    relay(2, 0)
+    project(3, 0)
+    combine_far(3, 0)
+    project(3, 1)
+    combine_near(3, 0)
+    combine_far(3, 1)
+    combine_near(3, 1)
+    relay(3, 0)
+    reduce(2, 0)
+    relay(3, 1)
+    reduce(3, 0)
+    reduce(3, 1)
+
     gathers = []
-    for j in (1, 3, 2):
-        there = lax.rem(chip + j, CHIPS)
-        gather_tx[j] = home[slot_at(there)]
-        copy = remote(gather_tx.at[j], out_ref.at[:, here], gather_send.at[j], gather_recv.at[j], along_chip(j))
-        copy.start()
-        gathers.append(copy)
-    out_ref[:, here] = home[slot_at(chip)]
+    for h in (0, 1):
+        for k in (1, 3, 2):
+            remote(
+                red.at[k, :, pl.ds(h * MID, MID)], homes[h].at[k], ret_send.at[k, h], ret_recv.at[k, h], along_wide(k)
+            ).wait_recv()
+        here = span(chip, h * MID, MID)
+        for j in (1, 3, 2):
+            gather_tx[h, j] = homes[h][slot_at(lax.rem(chip + j, CHIPS))]
+            copy = remote(
+                gather_tx.at[h, j], out_ref.at[:, here], gather_send.at[h, j], gather_recv.at[h, j], along_chip(j)
+            )
+            copy.start()
+            gathers.append(copy)
+        out_ref[:, here] = homes[h][slot_at(chip)]
 
     for k in (1, 2, 3):
         bnds[k].wait_send()
         packs[k].wait_send()
-    for s in range(4):
-        for i in range(4):
-            pairs[s, i].wait_send()
-        for i in range(6):
-            rs[s, i].wait_send()
-        if s:
-            returns[s].wait_send()
+    for copy in list(pairs.values()) + list(rs.values()) + list(returns.values()):
+        copy.wait_send()
     for copy in gathers:
         copy.wait_send()
         copy.wait_recv()
@@ -310,11 +361,13 @@
             pltpu.VMEM((4, 2, HALF, QUART // 2), BF16),
             pltpu.VMEM((4, 4, HALF, QUART // 2), BF16),
             pltpu.VMEM((4, HALF, QUART), BF16),
-            pltpu.VMEM((4, HALF, QUART), BF16),
-            pltpu.VMEM((4, HALF, QUART), BF16),
+            pltpu.VMEM((4, HALF, MID), BF16),
+            pltpu.VMEM((4, HALF, MID), BF16),
+            pltpu.VMEM((2, 4, HALF, MID), BF16),
             dma((5,)),
             dma((4,)), dma((4,)), dma((4,)), dma((4,)),
-            dma((4, 4)), dma((4, 4)), dma((4, 6)), dma((4, 6)), dma((4,)), dma((4,)), dma((4,)), dma((4,)),
+            dma((4, 2, 4)), dma((4, 2, 4)), dma((4, 2, 6)), dma((4, 2, 6)),
+            dma((4, 2)), dma((4, 2)), dma((2, 4)), dma((2, 4)),
         ],
         compiler_params=pltpu.CompilerParams(
             collective_id=1, has_side_effects=True, vmem_limit_bytes=60 * 1024 * 1024

time: 63.1 us -> 64.6 us (1.024)
  the two profiles are of different devices: /device:TPU:120 before, /device:TPU:32 now
where the time goes in v3:
time: 64.6 us; the launch traced here: 64.5 us
  Pallas kernels  62.6 us (97%)
  local copies, waits for them, and re-layouts  1.87 us (3%)
    pallas_call x1, Pallas kernels, body(): pl.pallas_call(kernel, out_shape=jax.ShapeDtypeStruct((HALF, D_OUT), BF16...  62.6 us
    unnamed x1, local copies, waits for them, and re-layouts  1.87 us

profile of v3, /device:TPU:32, one launch (start us, length us, event | category | flops | bytes accessed | tf_op | source)
XLA Modules:
  0.0 64.5 jit_solution(5722693405391028629)
XLA Ops:
  0.0 62.6 %shard_map.64 = bf16[64,4096]{1,0:T(8,128)(2,1)} custom-call(bf16[4,128,1024]{2,1,0:T(8,128)(2,1)} %bitcast.2, bf16[2,4,128,128]{3,2,1,0:T(8,128)(2,1)} %bitcast.3, bf16[2,2048,128]{2,1,0:T(8,128)(2,1)} %prompt_hbm.1, bf16[1024,4096]{1,0:T(8,128)(2,1)} %w_hbm.1, s32[4,4]{1,0:T(4,128)} %len_ref.1, s32[1,4]{1,0:T(1,128)} %gp_ref.1), custom_call_target="tpu_custom_call" | custom-call | flops 8999999488 | bytes 12582912 | tf_op jit(solution)/shard_map/pallas_call | solution.py:336
  62.6 1.9 %copy.8 = bf16[64,4096]{1,0:T(8,128)(2,1)} copy(bf16[64,4096]{1,0:T(8,128)(2,1)} %shard_map.64) | data formatting | bytes 1048576
